TPU v7x, 32 devices: a whole 2x2x4 slice. The times are simulated.
32 devices in a mesh: dp: 8 (over z, core), fsdp: 4 (over y, x).
Axes of the slice: x: 2, y: 2, z: 4, core: 2. Of those that a mesh axis runs over, the one named last changes fastest.
Arguments:
- hidden: bfloat16 [8192, 4096], P(('dp', 'fsdp')), may hold values from -6 to 6
- keys: bfloat16 [8192, 512], P(('dp', 'fsdp')), may hold values from -2.5 to 2.5
- queries: bfloat16 [512, 2048], P(('dp', 'fsdp')), may hold values from -2.5 to 2.5
- value_weight: bfloat16 [4096, 512], P('fsdp'), may hold values from -0.09375 to 0.09375
- adapter_down: bfloat16 [4096, 32], P('fsdp'), may hold values from -0.09375 to 0.09375
- adapter_up: bfloat16 [32, 512], replicated, may hold values from -1 to 1
- lengths: int32 [32, 16], P(('dp', 'fsdp')), may hold values from 1 to 32, as said below
- partner: int32 [512], P(('dp', 'fsdp')), may hold values from 0 to 511, as said below
Outputs:
- loss: float32 [], replicated
- adapter_down_grad: float32 [4096, 32], P('fsdp')
- adapter_up_grad: float32 [32, 512], replicated
Inputs may be any that keep to these rules, and one draw needn't show every extreme that they name: Each row holds the lengths of one device's 16 strings, laid one after another from its first token row, and they sum to 256. A permutation: partner[i] is the string paired with string i, never i itself.
All inputs are finite; a program needn't handle non-finite values.
Results may differ from a plain program's by a relative error of at most 0.024.
Values may be sent and summed in bfloat16 or wider, within the bound.
A program may use at most 64 MiB of HBM per device.

v0:
```python
import math

import jax
import jax.numpy as jnp
from jax import lax
from jax.sharding import PartitionSpec as P

HEADS = 16
KVH = 4
HD = 128


sharpness_divisor = 0.05


def shards(hidden, keys, queries, value_weight, adapter_down, adapter_up, lengths, partner):
    highest = lax.Precision.HIGHEST
    tok_rows = hidden.shape[0]
    strs = queries.shape[0]
    kv_width = value_weight.shape[1]
    emb_width = queries.shape[1]
    groups = HEADS // KVH
    n_fsdp = lax.axis_size("fsdp")
    n_dp = lax.axis_size("dp")
    columns = hidden
    base = jnp.dot(
        columns,
        lax.all_gather(value_weight, "fsdp", axis=0, tiled=True),
        preferred_element_type=jnp.float32,
    )
    low = jnp.dot(
        columns,
        lax.all_gather(adapter_down, "fsdp", axis=0, tiled=True),
        preferred_element_type=jnp.float32,
    )
    up_f = adapter_up.astype(jnp.float32)
    value = base + jnp.dot(low, up_f, precision=highest)
    length_row = lengths[0]
    ends = jnp.cumsum(length_row)
    starts = ends - length_row
    positions = jnp.arange(tok_rows)
    member = (
        (positions[None, :] >= starts[:, None]) & (positions[None, :] < ends[:, None])
    ).astype(jnp.float32)
    query_split = queries.reshape(strs, KVH, groups, HD)
    key_split = keys.reshape(tok_rows, KVH, HD)
    scores = jnp.einsum(
        "skgd,tkd->skgt", query_split, key_split, preferred_element_type=jnp.float32
    ) / math.sqrt(HD)
    raw = jnp.exp(scores) * member[:, None, None, :]
    probs = raw / jnp.sum(raw, axis=-1, keepdims=True)
    value_split = value.reshape(tok_rows, KVH, HD)
    pooled = jnp.einsum("skgt,tkd->skgd", probs, value_split, precision=highest).reshape(
        strs, emb_width
    )
    norm = jnp.sqrt(jnp.sum(pooled * pooled, axis=-1, keepdims=True) + 1e-06)
    unit = pooled / norm
    encoded_vectors = unit.astype(jnp.bfloat16)
    sample_count, row_partner = (
        lax.all_gather(encoded_vectors, "fsdp", axis=0, tiled=True),
        lax.all_gather(partner, "fsdp", axis=0, tiled=True),
    )
    cols = lax.all_gather(encoded_vectors, "dp", axis=0, tiled=True)
    dp_index = lax.axis_index("dp")
    fsdp_index = lax.axis_index("fsdp")
    row_ids = dp_index * (n_fsdp * strs) + jnp.arange(n_fsdp * strs)
    col_local = jnp.arange(n_dp * strs)
    col_ids = (col_local // strs * n_fsdp + fsdp_index) * strs + col_local % strs
    cosine_affinity_matrix = (
        lax.dot_general(
            sample_count, cols, (((1,), (1,)), ((), ())), preferred_element_type=jnp.float32
        )
        / sharpness_divisor
    )
    exponentiated_affinity = jnp.exp(cosine_affinity_matrix) * (
        row_ids[:, None] != col_ids[None, :]
    ).astype(jnp.float32)
    matching_pair_indicator = row_partner[:, None] == col_ids[None, :]
    normalizer_sums, positive = lax.psum(
        (
            jnp.sum(exponentiated_affinity, axis=1),
            jnp.sum(jnp.where(matching_pair_indicator, cosine_affinity_matrix, 0.0), axis=1),
        ),
        "fsdp",
    )
    own_totals = lax.dynamic_slice_in_dim(normalizer_sums, fsdp_index * strs, strs)
    own_positive = lax.dynamic_slice_in_dim(positive, fsdp_index * strs, strs)
    own_loss = jnp.sum(jnp.log(own_totals) - own_positive)
    affinity_derivative = (
        (
            exponentiated_affinity / normalizer_sums[:, None]
            - matching_pair_indicator.astype(jnp.float32)
        )
        / sharpness_divisor
    ).astype(jnp.bfloat16)
    picked = affinity_derivative
    row_part = lax.psum_scatter(
        jnp.dot(picked, cols, preferred_element_type=jnp.float32).astype(jnp.bfloat16),
        "fsdp",
        scatter_dimension=0,
        tiled=True,
    ).astype(jnp.float32)
    picked = affinity_derivative
    col_part = lax.psum_scatter(
        lax.dot_general(
            picked, sample_count, (((0,), (0,)), ((), ())), preferred_element_type=jnp.float32
        ).astype(jnp.bfloat16),
        "dp",
        scatter_dimension=0,
        tiled=True,
    ).astype(jnp.float32)
    grad_emb = row_part + col_part
    grad_pooled = (grad_emb - unit * jnp.sum(unit * grad_emb, axis=-1, keepdims=True)) / norm
    grad_split = grad_pooled.reshape(strs, KVH, groups, HD)
    grad_value = jnp.einsum("skgt,skgd->tkd", probs, grad_split, precision=highest).reshape(
        tok_rows, kv_width
    )
    up_part = lax.dot_general(low, grad_value, (((0,), (0,)), ((), ())), precision=highest)
    grad_low = lax.dot_general(
        grad_value, up_f, (((1,), (1,)), ((), ())), precision=highest
    ).astype(jnp.bfloat16)
    columns = hidden
    shard = lax.psum_scatter(
        lax.dot_general(
            columns, grad_low, (((0,), (0,)), ((), ())), preferred_element_type=jnp.float32
        ).astype(jnp.bfloat16),
        "fsdp",
        scatter_dimension=0,
        tiled=True,
    )
    down_grad = lax.psum(shard, "dp").astype(jnp.float32)
    up_grad, loss_sum = lax.psum((up_part, own_loss), ("dp", "fsdp"))
    loss = loss_sum / (strs * n_dp * n_fsdp)
    return (loss, down_grad, up_grad)


def solution(mesh):
    placed = (
        P(("dp", "fsdp"), None),
        P(("dp", "fsdp"), None),
        P(("dp", "fsdp"), None),
        P("fsdp", None),
        P("fsdp", None),
        P(),
        P(("dp", "fsdp"), None),
        P(("dp", "fsdp")),
    )
    return jax.shard_map(
        shards, mesh=mesh, in_specs=placed, out_specs=(P(), P("fsdp", None), P()), check_vma=False
    )
```

profile of v0, /device:TPU:0, one launch (start us, length us, event | category | flops | bytes accessed | tf_op | source)
XLA Modules:
  0.0 378.0 jit_solution(491556810204138193)
XLA Ops:
  8.9 0.9 reshape.128
  9.7 1.0 reshape.127
  10.8 1.2 dynamic-slice
  13.5 8.8 %all-reduce = s32[64]{0:T(128)S(1)} all-reduce(s32[64]{0:T(128)S(1)} %dynamic-update-slice), channel_id=1, replica_groups=mesh['dp'=8,'fsdp'=4] {'fsdp'}, use_global_device_ids=true, to_apply=%add | all-reduce | flops 64 | bytes 512
  22.4 11.3 %all_gather.16 = bf16[4096,32]{0,1:T(8,128)(2,1)S(1)} all-gather(bf16[1024,32]{0,1:T(8,128)(2,1)} %param.12), channel_id=1, replica_groups=mesh['dp'=8,'fsdp'=4] {'fsdp'}, dimensions={0}, use_global_device_ids=true | all-gather | bytes 327680 | tf_op jit(solution)/shard_map/all_gather | solution.py:33
  34.9 32.5 %all-gather.2.cloned.1.call-done = bf16[4096,512]{1,0:T(8,128)(2,1)} async-done(((bf16[1024,512]{1,0:T(8,128)(2,1)}), bf16[4096,512]{1,0:T(8,128)(2,1)}) %all-gather.2.cloned.1.call-update) | async-done | bytes 4194320 | tf_op jit(solution)/shard_map/all_gather | solution.py:28
  67.4 3.4 fusion.29
  72.3 8.9 %all_gather.17 = bf16[64,2048]{1,0:T(8,128)(2,1)S(1)} all-gather(bf16[16,2048]{1,0:T(8,128)(2,1)S(1)} %fusion.24), channel_id=1, replica_groups=mesh['dp'=8,'fsdp'=4] {'fsdp'}, dimensions={0}, use_global_device_ids=true | all-gather | bytes 327680 | tf_op jit(solution)/shard_map/all_gather | solution.py:60
  81.2 14.9 %all_gather.18 = bf16[128,2048]{1,0:T(8,128)(2,1)S(1)} all-gather(bf16[16,2048]{1,0:T(8,128)(2,1)S(1)} %fusion.24), channel_id=1, replica_groups=mesh['dp'=8,'fsdp'=4] {'dp'}, dimensions={0}, use_global_device_ids=true | all-gather | bytes 589824 | tf_op jit(solution)/shard_map/all_gather | solution.py:63
  96.5 8.9 %all-reduce.1 = (f32[64]{0:T(128)S(1)}, f32[64]{0:T(128)S(1)}) all-reduce(f32[64]{0:T(128)S(1)} %get-tuple-element.4, f32[64]{0:T(128)S(1)} %get-tuple-element.3), channel_id=1, replica_groups=mesh['dp'=8,'fsdp'=4] {'fsdp'}, use_global_device_ids=true, to_apply=%region_6.7 | all-reduce | flops 128 | bytes 1024 | tf_op jit(solution)/shard_map/psum | solution.py:79
  105.4 1.0 convolution_convert_fusion.2
  106.5 1.2 convolution_convert_fusion.1
  107.8 22.0 %reduce-scatter.4.cloned.1.call-done = bf16[16,2048]{1,0:T(8,128)(2,1)} async-done(((bf16[64,2048]{1,0:T(8,128)(2,1)}), bf16[16,2048]{1,0:T(8,128)(2,1)}) %reduce-scatter.4.cloned.1.call-update) | async-done | bytes 65552 | tf_op jit(solution)/shard_map/reduce_scatter | solution.py:97
  129.7 33.4 %reduce-scatter.6.cloned.1.call-done = bf16[16,2048]{1,0:T(8,128)(2,1)} async-done(((bf16[128,2048]{1,0:T(8,128)(2,1)}), bf16[16,2048]{1,0:T(8,128)(2,1)}) %reduce-scatter.6.cloned.1.call-update) | async-done | bytes 65552 | tf_op jit(solution)/shard_map/reduce_scatter | solution.py:104
  163.1 1.1 multiply_reduce_fusion
  164.2 1.0 subtract_divide_fusion
  166.5 1.2 fusion
  167.8 22.3 %reduce-scatter.8.cloned.1.call-done = bf16[1024,32]{0,1:T(8,128)(2,1)} async-done(((bf16[4096,32]{0,1:T(8,128)(2,1)}), bf16[1024,32]{0,1:T(8,128)(2,1)}) %reduce-scatter.8.cloned.1.call-update) | async-done | bytes 65552 | tf_op jit(solution)/shard_map/reduce_scatter | solution.py:123
  190.1 1.2 fusion.31
  192.0 39.5 %psum.37 = f32[]{:T(128)} all-reduce(f32[]{:T(128)} %subtract_reduce_fusion), channel_id=1, replica_groups=mesh['dp'=8,'fsdp'=4] {'dp','fsdp'}, use_global_device_ids=true, to_apply=%region_8.9 | all-reduce | flops 1 | bytes 8 | tf_op jit(solution)/shard_map/psum | solution.py:132
  232.2 13.8 %all-reduce.5.cloned.1.call-done = bf16[1024,32]{0,1:T(8,128)(2,1)} async-done(((bf16[1024,32]{0,1:T(8,128)(2,1)}), bf16[1024,32]{0,1:T(8,128)(2,1)}) %all-reduce.5.cloned.1.call-update) | async-done | bytes 65552 | tf_op jit(solution)/shard_map/psum | solution.py:131
  246.0 1.5 convert_element_type.53
  247.5 121.1 %all-reduce.7.cloned.1.call-done = f32[32,512]{1,0:T(8,128)} async-done(((f32[32,512]{1,0:T(8,128)}), f32[32,512]{1,0:T(8,128)}) %all-reduce.7.cloned.1.call-update) | async-done | bytes 65552 | tf_op jit(solution)/shard_map/psum | solution.py:132
  368.6 1.5 copy.46
  (41 shorter events, 7.7 us)
Async XLA Ops:
  7.2 27.0 %copy-start = (bf16[256,4096]{1,0:T(8,128)(2,1)S(1)}, bf16[256,4096]{1,0:T(8,128)(2,1)}, u32[]{:S(2)}) copy-start(bf16[256,4096]{1,0:T(8,128)(2,1)} %param.8) | copy-start | bytes 6291460
  7.2 26.5 %copy-start.2 = (s32[1,16]{1,0:T(1,128)S(1)}, s32[1,16]{1,0:T(1,128)}, u32[]{:S(2)}) copy-start(s32[1,16]{1,0:T(1,128)} %param.14) | copy-start | bytes 196
  7.2 60.2 %all-gather.2.cloned.1.call-start = ((), (), s32[]{:S(2)}) async-start(), calls=%async_computation.3 | async-start | bytes 5242880 | tf_op jit(solution)/shard_map/all_gather | solution.py:28
  7.9 121.8 %reduce-scatter.4.cloned.1.call-start = ((), (), s32[]{:S(2)}) async-start(), calls=%async_computation.4 | async-start | bytes 327680 | tf_op jit(solution)/shard_map/reduce_scatter | solution.py:97
  34.9 36.0 %copy-start.1 = (bf16[32,512]{1,0:T(8,128)(2,1)S(1)}, bf16[32,512]{1,0:T(8,128)(2,1)}, u32[]{:S(2)}) copy-start(bf16[32,512]{1,0:T(8,128)(2,1)} %param.13) | copy-start | bytes 98308
  106.5 56.7 %reduce-scatter.6.cloned.1.call-start = ((), (), s32[]{:S(2)}) async-start(), calls=%async_computation.5 | async-start | bytes 589824 | tf_op jit(solution)/shard_map/reduce_scatter | solution.py:104
  107.7 82.3 %reduce-scatter.8.cloned.1.call-start = ((), (), s32[]{:S(2)}) async-start(), calls=%async_computation.6 | async-start | bytes 327680 | tf_op jit(solution)/shard_map/reduce_scatter | solution.py:123
  167.7 78.3 %all-reduce.5.cloned.1.call-start = ((), (), s32[]{:S(2)}) async-start(), calls=%async_computation.7 | async-start | bytes 131072 | tf_op jit(solution)/shard_map/psum | solution.py:131
  190.1 178.5 %all-reduce.7.cloned.1.call-start = ((), (), s32[]{:S(2)}) async-start(), calls=%async_computation.8 | async-start | bytes 131072 | tf_op jit(solution)/shard_map/psum | solution.py:132
Sparse Core Ops, SparseCore 0:
  9.9 57.4 all-gather.1
  106.6 23.1 reduce-scatter.3
  132.1 30.9 reduce-scatter.5
  167.8 22.1 reduce-scatter.7
  192.3 53.6 all-reduce.4
  252.0 116.5 all-reduce.6
where the time goes:
time: 380 us; the launch traced here: 378 us
  waiting for transfers between devices  246 us (65%)
  blocking collectives  92.5 us (24%)
  between operations  16.7 us (4%)
  matrix products  11.7 us (3%)
  local copies, waits for them, and re-layouts  6.62 us (2%)
  other arithmetic  4.56 us (1%)
    psum x1, waiting for transfers between devices, shards(): up_grad, loss_sum = lax.psum((up_part, own_loss), ('dp', 'fsdp'))  121 us
    psum x1, blocking collectives, shards(): up_grad, loss_sum = lax.psum((up_part, own_loss), ('dp', 'fsdp'))  39.5 us
    reduce_scatter x1, waiting for transfers between devices, shards(): lax.psum_scatter(lax.dot_general(picked, sample_count, (((0,), (0,)), (()...  33.4 us
    all_gather x1, waiting for transfers between devices, shards(): lax.all_gather(value_weight, 'fsdp', axis=0, tiled=True)  32.5 us
    reduce_scatter x1, waiting for transfers between devices, shards(): lax.psum_scatter(lax.dot_general(columns, grad_low, (((0,), (0,)), ((), (...  22.3 us
    reduce_scatter x1, waiting for transfers between devices, shards(): lax.psum_scatter(jnp.dot(picked, cols, preferred_element_type=jnp.float32...  22 us
    all_gather x1, blocking collectives, shards(): cols = lax.all_gather(encoded_vectors, 'dp', axis=0, tiled=True)  14.9 us
    psum x1, waiting for transfers between devices, shards(): down_grad = lax.psum(shard, 'dp').astype(jnp.float32)  13.8 us
  transfers between devices with their start and end apart: 6, of which 6 were waited for; matrix products, arithmetic and copies ran while one was open for 3% of the time, Pallas kernels for 0%

commit v1 on v0

--- a/solution.py
+++ b/solution.py
@@ -1,8 +1,11 @@
+import functools
 import math
 
 import jax
 import jax.numpy as jnp
 from jax import lax
+from jax.experimental import pallas as pl
+from jax.experimental.pallas import tpu as pltpu
 from jax.sharding import PartitionSpec as P
 
 HEADS = 16
@@ -134,6 +137,414 @@
     return (loss, down_grad, up_grad)
 
 
+LANES = 128
+MESH = pl.DeviceIdType.MESH
+HIGHEST = lax.Precision.HIGHEST
+
+
+def dot(x, y, cx, cy, precision=None):
+    return lax.dot_general(
+        x, y, (((cx,), (cy,)), ((), ())), precision=precision, preferred_element_type=jnp.float32
+    )
+
+
+def fits(hidden, keys, queries, value_weight, adapter_down, adapter_up, lengths, partner):
+    n_dp, n_fsdp = lax.axis_size("dp"), lax.axis_size("fsdp")
+    strings = n_dp * n_fsdp * queries.shape[0]
+    rank, width = adapter_up.shape
+    return (
+        n_fsdp == 4
+        and n_dp % 2 == 0
+        and strings <= 1024
+        and queries.shape[0] == 16
+        and (rank // 16) * (width // LANES) == n_dp
+        and hidden.shape[1] == n_dp * n_fsdp * LANES
+    )
+
+
+def fused(
+    n_dp,
+    hidden_ref,
+    keys_ref,
+    queries_ref,
+    weight_ref,
+    down_in_ref,
+    up_ref,
+    len_ref,
+    partner_ref,
+    loss_ref,
+    down_ref,
+    up_out_ref,
+    w_all,
+    acc,
+    low_t,
+    probs,
+    emb_all,
+    unit_ref,
+    totals,
+    msg,
+    got1,
+    sum1,
+    got2,
+    sum2,
+    got3,
+    final,
+    send_sem,
+    w_sem,
+    e_sem,
+    g_sem,
+):
+    f32, bf16 = jnp.float32, jnp.bfloat16
+    a, f = lax.axis_index("dp"), lax.axis_index("fsdp")
+    nz = n_dp // 2
+    z, k = a // 2, a % 2
+    other = 1 - k
+    xn = f + 1 - 2 * (f % 2)
+    yn = (f + 2) % 4
+    dn = (xn + 2) % 4
+    pair_dev = (z * 2 + other, f)
+    x_dev, y_dev, d_dev = (a, xn), (a, yn), (a, dn)
+    z_list = [(z + r) % nz for r in range(nz)]
+    z_devs = [(zz * 2 + k, f) for zz in z_list]
+
+    barrier = pltpu.get_barrier_semaphore()
+    peers = [pair_dev, x_dev, y_dev, d_dev] + z_devs[1:]
+    for dev in peers:
+        pl.semaphore_signal(barrier, inc=1, device_id=dev, device_id_type=MESH)
+
+    tok, strs = hidden_ref.shape[0], queries_ref.shape[0]
+    rank, width = up_ref.shape
+    emb_w = queries_ref.shape[1]
+    groups = HEADS // KVH
+    half = weight_ref.shape[0] // 2
+    piece = (half + rank) // 2
+    strings = emb_all.shape[0]
+
+    eye = (
+        lax.broadcasted_iota(jnp.int32, (rank, rank), 0)
+        == lax.broadcasted_iota(jnp.int32, (rank, rank), 1)
+    ).astype(bf16)
+    for h in range(2):
+        w_all[f, h, 0:half, :] = weight_ref[h * half : (h + 1) * half, :]
+        w_all[f, h, half : half + rank, :] = dot(
+            eye, down_in_ref[h * half : (h + 1) * half, :], 1, 1
+        ).astype(bf16)
+    pl.semaphore_wait(barrier, len(peers))
+
+    sends = []
+
+    def push(src, dst, recv, dev):
+        copy = pltpu.make_async_remote_copy(
+            src_ref=src,
+            dst_ref=dst,
+            send_sem=send_sem.at[len(sends)],
+            recv_sem=recv,
+            device_id=dev,
+            device_id_type=MESH,
+        )
+        copy.start()
+        sends.append(copy)
+
+    def arrive(dst, recv):
+        pltpu.make_async_remote_copy(
+            src_ref=dst,
+            dst_ref=dst,
+            send_sem=send_sem.at[0],
+            recv_sem=recv,
+            device_id=pair_dev,
+            device_id_type=MESH,
+        ).wait_recv()
+
+    def w_slot(s, h, c):
+        return w_all.at[s, h, pl.ds(c * piece, piece), :], w_sem.at[s, h, c]
+
+    def w_push(s, c, dev):
+        ref, sem = w_slot(s, k, c)
+        push(ref, ref, sem, dev)
+
+    def w_arrive(s, h, c):
+        arrive(*w_slot(s, h, c))
+
+    w_push(f, 0, x_dev)
+    w_push(f, 1, y_dev)
+    w_push(f, 1, x_dev)
+    w_push(f, 0, y_dev)
+
+    rows = groups * strs
+    row_str = lax.broadcasted_iota(jnp.int32, (rows, strs), 0) % strs
+    lane_str = lax.broadcasted_iota(jnp.int32, (rows, strs), 1)
+    len_f = jnp.broadcast_to(len_ref[...].astype(f32), (rows, strs))
+    ends = jnp.sum(jnp.where(lane_str <= row_str, len_f, 0.0), axis=1, keepdims=True)
+    starts = jnp.sum(jnp.where(lane_str < row_str, len_f, 0.0), axis=1, keepdims=True)
+    at = lax.broadcasted_iota(jnp.int32, (rows, tok), 1).astype(f32)
+    member = (at >= starts) & (at < ends)
+    for kv in range(KVH):
+        q = jnp.concatenate(
+            [
+                queries_ref[:, (kv * groups + g) * HD : (kv * groups + g + 1) * HD]
+                for g in range(groups)
+            ],
+            axis=0,
+        )
+        scores = dot(q, keys_ref[:, kv * HD : (kv + 1) * HD], 1, 1) / math.sqrt(HD)
+        raw = jnp.where(member, jnp.exp(scores), 0.0)
+        probs[kv] = raw / jnp.sum(raw, axis=1, keepdims=True)
+
+    acc[...] = jnp.zeros_like(acc)
+    low_t[...] = jnp.zeros_like(low_t)
+
+    def project(s, h):
+        x = hidden_ref[:, pl.ds(pl.multiple_of((2 * s + h) * half, half), half)]
+        acc[...] += dot(x, w_all[s, h, 0:half, :], 1, 0)
+        low_t[...] += dot(w_all[s, h, half : half + rank, :], x, 1, 1)
+
+    project(f, 0)
+    project(f, 1)
+    w_arrive(xn, k, 0)
+    w_push(xn, 0, y_dev)
+    w_push(xn, 0, pair_dev)
+    w_arrive(yn, k, 1)
+    w_push(yn, 1, x_dev)
+    w_push(yn, 1, pair_dev)
+    w_arrive(xn, k, 1)
+    w_push(xn, 1, pair_dev)
+    w_arrive(yn, k, 0)
+    w_push(yn, 0, pair_dev)
+    project(xn, k)
+    project(yn, k)
+    for s in (xn, yn):
+        for c in range(2):
+            w_arrive(s, other, c)
+        project(s, other)
+    for c in range(2):
+        w_arrive(dn, k, c)
+        w_push(dn, c, pair_dev)
+    project(dn, k)
+    for c in range(2):
+        w_arrive(dn, other, c)
+    project(dn, other)
+
+    up_f = up_ref[...].astype(f32)
+    value = acc[...] + dot(low_t[...], up_f, 0, 0, HIGHEST)
+    square = jnp.zeros((strs, 1), f32)
+    for kv in range(KVH):
+        pooled = dot(probs[kv], value[:, kv * HD : (kv + 1) * HD], 1, 0, HIGHEST)
+        for g in range(groups):
+            part = pooled[g * strs : (g + 1) * strs, :]
+            unit_ref[:, (kv * groups + g) * HD : (kv * groups + g + 1) * HD] = part
+            square += jnp.sum(part * part, axis=1, keepdims=True)
+    norm = jnp.sqrt(square + 1e-06)
+    unit = unit_ref[...] / norm
+    unit_ref[...] = unit
+    emb = unit.astype(bf16)
+
+    def block_of(zz, kk, ff):
+        d = (zz * 2 + kk) * 4 + ff
+        return emb_all.at[pl.ds(pl.multiple_of(d * strs, strs), strs), :], e_sem.at[d]
+
+    mine = (a * 4 + f) * strs
+    own_rows = pl.ds(pl.multiple_of(mine, strs), strs)
+    emb_all[own_rows, 0:emb_w] = emb
+    partner_row = partner_ref[...].astype(f32)
+    own_partner = jnp.sum(
+        jnp.where(
+            lax.broadcasted_iota(jnp.int32, (strs, strs), 0)
+            == lax.broadcasted_iota(jnp.int32, (strs, strs), 1),
+            jnp.broadcast_to(partner_row, (strs, strs)),
+            0.0,
+        ),
+        axis=1,
+        keepdims=True,
+    )
+    high = jnp.floor(own_partner * (1.0 / 256.0))
+    lane = lax.broadcasted_iota(jnp.int32, (strs, LANES), 1)
+    emb_all[own_rows, emb_w : emb_w + LANES] = jnp.where(
+        lane == 0, own_partner - 256.0 * high, jnp.where(lane == 1, high, 0.0)
+    ).astype(bf16)
+
+    def e_push(blk, dev):
+        push(blk[0], blk[0], blk[1], dev)
+
+    own_block = block_of(z, k, f)
+    for dev in z_devs[1:]:
+        e_push(own_block, dev)
+    for dev in (x_dev, y_dev, pair_dev):
+        e_push(own_block, dev)
+    for r in range(1, nz):
+        blk = block_of(z_list[r], k, f)
+        arrive(*blk)
+        for dev in (x_dev, y_dev, pair_dev):
+            e_push(blk, dev)
+    for r in range(nz):
+        for s, relay in ((xn, y_dev), (yn, x_dev)):
+            blk = block_of(z_list[r], k, s)
+            arrive(*blk)
+            if (r % 2 == 0) == (s is xn):
+                e_push(blk, relay)
+            e_push(blk, pair_dev)
+    for r in range(nz):
+        blk = block_of(z_list[r], k, dn)
+        arrive(*blk)
+        e_push(blk, pair_dev)
+    for r in range(nz):
+        for s in (f, xn, yn, dn):
+            arrive(*block_of(z_list[r], other, s))
+
+    step = min(strings, 128)
+
+    def rows_of(i, loss):
+        here = pl.ds(pl.multiple_of(i * step, step), step)
+        logits = dot(emb_all[here, 0:emb_w], emb_all[:, 0:emb_w], 1, 1) / sharpness_divisor
+        row = i * step + lax.broadcasted_iota(jnp.int32, (step, strings), 0)
+        col = lax.broadcasted_iota(jnp.int32, (step, strings), 1)
+        total = jnp.sum(jnp.where(row != col, jnp.exp(logits), 0.0), axis=1, keepdims=True)
+        totals[here, :] = jnp.broadcast_to(total, (step, LANES))
+        code = emb_all[here, emb_w : emb_w + LANES].astype(f32)
+        mate = code[:, 0:1] + 256.0 * code[:, 1:2]
+        positive = jnp.sum(
+            jnp.where(mate == col.astype(f32), logits, 0.0), axis=1, keepdims=True
+        )
+        return loss + jnp.sum(jnp.log(total) - positive, axis=0, keepdims=True)
+
+    loss = lax.fori_loop(0, strings // step, rows_of, jnp.zeros((1, 1), f32))
+    loss_ref[...] = jnp.broadcast_to(loss / strings, loss_ref.shape)
+
+    logits = dot(emb_all[:, 0:emb_w], emb, 1, 1) / sharpness_divisor
+    j = lax.broadcasted_iota(jnp.int32, (strings, strs), 0)
+    i = mine + lax.broadcasted_iota(jnp.int32, (strings, strs), 1)
+    expd = jnp.where(i != j, jnp.exp(logits), 0.0)
+    own_total = jnp.sum(expd, axis=0, keepdims=True)
+    own_hit = jnp.where(partner_row == j.astype(f32), 1.0, 0.0)
+    code = emb_all[:, emb_w : emb_w + LANES].astype(f32)
+    mate = code[:, 0:1] + 256.0 * code[:, 1:2]
+    hit = jnp.where(mate == i.astype(f32), 1.0, 0.0)
+    row_grad = ((expd / own_total - own_hit) / sharpness_divisor).astype(bf16)
+    col_grad = ((expd / totals[:, 0:1] - hit) / sharpness_divisor).astype(bf16)
+    every = emb_all[:, 0:emb_w]
+    grad_emb = dot(row_grad, every, 0, 0) + dot(col_grad, every, 0, 0)
+    unit = unit_ref[...]
+    grad_pooled = (grad_emb - unit * jnp.sum(unit * grad_emb, axis=1, keepdims=True)) / norm
+
+    for kv in range(KVH):
+        g_kv = jnp.concatenate(
+            [
+                grad_pooled[:, (kv * groups + g) * HD : (kv * groups + g + 1) * HD]
+                for g in range(groups)
+            ],
+            axis=0,
+        )
+        acc[:, kv * HD : (kv + 1) * HD] = dot(probs[kv], g_kv, 0, 0, HIGHEST)
+    grad_value = acc[...]
+    up_part = dot(low_t[...], grad_value, 1, 0, HIGHEST).astype(bf16)
+    grad_low_t = dot(up_f, grad_value, 1, 1, HIGHEST).astype(bf16)
+
+    per_row = width // LANES
+    span = n_dp * LANES
+    for ff in range(4):
+        part = dot(grad_low_t, hidden_ref[:, ff * span : (ff + 1) * span], 1, 0).astype(bf16)
+        for aa in range(n_dp):
+            msg[aa % 2, ff, aa // 2, 0:rank, :] = part[:, aa * LANES : (aa + 1) * LANES]
+            r0, c0 = aa // per_row * 16, aa % per_row * LANES
+            msg[aa % 2, ff, aa // 2, rank : rank + 16, :] = up_part[r0 : r0 + 16, c0 : c0 + LANES]
+
+    push(msg.at[other], got1, g_sem.at[0], pair_dev)
+    arrive(got1, g_sem.at[0])
+    sum1[...] = (msg[k].astype(f32) + got1[...].astype(f32)).astype(bf16)
+    for n, (s, dev) in enumerate(((xn, x_dev), (yn, y_dev), (dn, d_dev))):
+        push(sum1.at[s], got2.at[f], g_sem.at[1 + f], dev)
+    got2[f] = sum1[f]
+    for s in (xn, yn, dn):
+        arrive(got2.at[s], g_sem.at[1 + s])
+    total2 = got2[0].astype(f32)
+    for s in range(1, 4):
+        total2 += got2[s].astype(f32)
+    sum2[...] = total2.astype(bf16)
+    for r in range(1, nz):
+        push(sum2.at[z_list[r]], got3.at[z], g_sem.at[5 + z], z_devs[r])
+    got3[z] = sum2[z]
+    for r in range(1, nz):
+        arrive(got3.at[z_list[r]], g_sem.at[5 + z_list[r]])
+    total3 = got3[0].astype(f32)
+    for s in range(1, nz):
+        total3 += got3[s].astype(f32)
+    final[k, z] = total3.astype(bf16)
+    fin = final.at[k, z]
+    base = 5 + nz
+    for dev in z_devs[1:] + [pair_dev]:
+        push(fin, fin, g_sem.at[base + a], dev)
+    for r in range(1, nz):
+        slot, sem = final.at[k, z_list[r]], g_sem.at[base + z_list[r] * 2 + k]
+        arrive(slot, sem)
+        push(slot, slot, sem, pair_dev)
+    for r in range(nz):
+        arrive(final.at[other, z_list[r]], g_sem.at[base + z_list[r] * 2 + other])
+    for aa in range(n_dp):
+        r0, c0 = aa // per_row * 16, aa % per_row * LANES
+        down_ref[:, aa * LANES : (aa + 1) * LANES] = final[aa % 2, aa // 2, 0:rank, :].astype(f32)
+        up_out_ref[r0 : r0 + 16, c0 : c0 + LANES] = final[
+            aa % 2, aa // 2, rank : rank + 16, :
+        ].astype(f32)
+    for copy in sends:
+        copy.wait_send()
+
+
+def fused_shards(hidden, keys, queries, value_weight, adapter_down, adapter_up, lengths, partner):
+    n_dp, n_fsdp = lax.axis_size("dp"), lax.axis_size("fsdp")
+    tok, depth = hidden.shape
+    strs, emb_w = queries.shape
+    shard, width = value_weight.shape
+    rank = adapter_up.shape[0]
+    nz = n_dp // 2
+    strings = n_dp * n_fsdp * strs
+    f32, bf16 = jnp.float32, jnp.bfloat16
+    tall = rank + 16
+    vmem = pl.BlockSpec(memory_space=pltpu.VMEM)
+    blocks = n_dp * n_fsdp
+    loss, down_t, up_grad = pl.pallas_call(
+        functools.partial(fused, n_dp),
+        out_shape=(
+            jax.ShapeDtypeStruct((8, LANES), f32),
+            jax.ShapeDtypeStruct((rank, shard), f32),
+            jax.ShapeDtypeStruct((rank, width), f32),
+        ),
+        in_specs=[vmem] * 8,
+        out_specs=(vmem,) * 3,
+        scratch_shapes=[
+            pltpu.VMEM((n_fsdp, 2, shard // 2 + rank, width), bf16),
+            pltpu.VMEM((tok, width), f32),
+            pltpu.VMEM((rank, tok), f32),
+            pltpu.VMEM((KVH, strs * HEADS // KVH, tok), f32),
+            pltpu.VMEM((strings, emb_w + LANES), bf16),
+            pltpu.VMEM((strs, emb_w), f32),
+            pltpu.VMEM((strings, LANES), f32),
+            pltpu.VMEM((2, n_fsdp, nz, tall, LANES), bf16),
+            pltpu.VMEM((n_fsdp, nz, tall, LANES), bf16),
+            pltpu.VMEM((n_fsdp, nz, tall, LANES), bf16),
+            pltpu.VMEM((n_fsdp, nz, tall, LANES), bf16),
+            pltpu.VMEM((nz, tall, LANES), bf16),
+            pltpu.VMEM((nz, tall, LANES), bf16),
+            pltpu.VMEM((2, nz, tall, LANES), bf16),
+            pltpu.SemaphoreType.DMA((64 + 4 * n_dp,)),
+            pltpu.SemaphoreType.DMA((n_fsdp, 2, 2)),
+            pltpu.SemaphoreType.DMA((blocks,)),
+            pltpu.SemaphoreType.DMA((5 + nz + n_dp,)),
+        ],
+        compiler_params=pltpu.CompilerParams(
+            collective_id=0, has_side_effects=True, vmem_limit_bytes=48 * 1024 * 1024
+        ),
+    )(
+        hidden,
+        keys,
+        queries,
+        value_weight,
+        adapter_down,
+        adapter_up,
+        lengths,
+        partner.reshape(1, strs),
+    )
+    return (loss[0, 0], down_t.T, up_grad)
+
+
 def solution(mesh):
     placed = (
         P(("dp", "fsdp"), None),
@@ -145,6 +556,10 @@
         P(("dp", "fsdp"), None),
         P(("dp", "fsdp")),
     )
+
+    def body(*args):
+        return (fused_shards if fits(*args) else shards)(*args)
+
     return jax.shard_map(
-        shards, mesh=mesh, in_specs=placed, out_specs=(P(), P("fsdp", None), P()), check_vma=False
-    )
+        body, mesh=mesh, in_specs=placed, out_specs=(P(), P("fsdp", None), P()), check_vma=False
+    )

time: 380 us -> 79 us (0.21)
  waiting for transfers between devices: 246 us -> 0 us
  blocking collectives: 92.5 us -> 0 us
  Pallas kernels: 0 us -> 68.5 us
  between operations: 16.7 us -> 0.66 us
  matrix products: 11.7 us -> 0 us
  other arithmetic: 4.56 us -> 0 us
    psum x2 -> x0, waiting for transfers between devices: 135 us -> none  [the longest x1 121 us: shards(): up_grad, loss_sum = lax.psum((up_part, own_loss), ('dp', 'fsdp'))]
    reduce_scatter x3 -> x0, waiting for transfers between devices: 77.6 us -> none  [the longest x1 33.4 us: shards(): lax.psum_scatter(lax.dot_general(picked, sample_count, (((0,), (0,)), (()...]
    pallas_call x0 -> x1, Pallas kernels: none -> 68.5 us  [fused_shards(): pl.pallas_call(functools.partial(fused, n_dp), out_shape=(jax.ShapeDtypeS...]
    psum x2 -> x0, blocking collectives: 48.5 us -> none  [the longest x1 39.5 us: shards(): up_grad, loss_sum = lax.psum((up_part, own_loss), ('dp', 'fsdp'))]
    all_gather x3 -> x0, blocking collectives: 35.2 us -> none  [the longest x1 14.9 us: shards(): cols = lax.all_gather(encoded_vectors, 'dp', axis=0, tiled=True)]
    all_gather x1 -> x0, waiting for transfers between devices: 32.5 us -> none  [shards(): lax.all_gather(value_weight, 'fsdp', axis=0, tiled=True)]
    dot_general x11 -> x0, matrix products: 11.4 us -> none  [the longest x1 3.42 us: shards(): jnp.dot(columns, lax.all_gather(value_weight, 'fsdp', axis=0, tiled=True)...]
    unnamed x1 -> x0, blocking collectives: 8.82 us -> none
  transfers between devices with their start and end apart: 6 -> 0, of which waited for: 6 -> 0; matrix products, arithmetic and copies ran while one was open for 3% -> 0% of each run, Pallas kernels for 0% -> 0%
where the time goes in v1:
time: 79 us; the launch traced here: 78.6 us
  Pallas kernels  68.5 us (87%)
  local copies, waits for them, and re-layouts  9.47 us (12%)
    pallas_call x1, Pallas kernels, fused_shards(): pl.pallas_call(functools.partial(fused, n_dp), out_shape=(jax.ShapeDtypeS...  68.5 us
    unnamed x17, local copies, waits for them, and re-layouts  8.96 us

profile of v1, /device:TPU:0, one launch (start us, length us, event | category | flops | bytes accessed | tf_op | source)
XLA Modules:
  0.0 78.6 jit_solution(2374465927297030707)
XLA Ops:
  0.6 1.0 %copy.11.down_in_ref = bf16[1024,32]{1,0:T(8,128)(2,1)S(1)} copy(bf16[1024,32]{0,1:T(8,128)(2,1)} %param.12) | data formatting | bytes 131072 | tf_op args[4]
  1.6 0.0 copy-start
  1.7 1.6 %copy-done = bf16[256,4096]{1,0:T(8,128)(2,1)S(1)} copy-done((bf16[256,4096]{1,0:T(8,128)(2,1)S(1)}, bf16[256,4096]{1,0:T(8,128)(2,1)}, u32[]{:S(2)}) %copy-start) | copy-done | bytes 2097176
  3.2 0.0 copy-start.1
  3.2 1.2 %copy-done.1 = bf16[1024,512]{1,0:T(8,128)(2,1)S(1)} copy-done((bf16[1024,512]{1,0:T(8,128)(2,1)S(1)}, bf16[1024,512]{1,0:T(8,128)(2,1)}, u32[]{:S(2)}) %copy-start.1) | copy-done | bytes 1048600
  4.5 0.0 copy-start.2
  4.5 0.9 %copy-done.2 = bf16[256,512]{1,0:T(8,128)(2,1)S(1)} copy-done((bf16[256,512]{1,0:T(8,128)(2,1)S(1)}, bf16[256,512]{1,0:T(8,128)(2,1)}, u32[]{:S(2)}) %copy-start.2) | copy-done | bytes 262168
  5.4 0.0 copy-start.3
  5.4 0.8 %copy-done.3 = bf16[16,2048]{1,0:T(8,128)(2,1)S(1)} copy-done((bf16[16,2048]{1,0:T(8,128)(2,1)S(1)}, bf16[16,2048]{1,0:T(8,128)(2,1)}, u32[]{:S(2)}) %copy-start.3) | copy-done | bytes 65560
  6.3 0.0 copy-start.4
  6.3 0.8 copy-done.4
  7.0 0.0 copy-start.5
  7.0 0.7 copy-done.5
  7.7 0.0 copy-start.6
  7.7 0.7 copy-done.6
  8.3 68.5 %shard_map.103 = (f32[8,128]{1,0:T(8,128)S(1)}, f32[32,1024]{1,0:T(8,128)S(1)}, f32[32,512]{1,0:T(8,128)S(1)}) custom-call(bf16[256,4096]{1,0:T(8,128)(2,1)S(1)} %copy-done, bf16[256,512]{1,0:T(8,128)(2,1)S(1)} %copy-done.2, bf16[16,2048]{1,0:T(8,128)(2,1)S(1)} %copy-done.3, bf16[1024,512]{1,0:T(8,128)(2,1)S(1)} %copy-done.1, ...), custom_call_target="tpu_custom_call" | custom-call | tf_op jit(solution)/shard_map/pallas_call | solution.py:503
  76.8 0.5 slice.3
  77.3 0.7 copy.14
  78.0 0.6 copy.15
Async XLA Ops:
  1.6 1.6 %copy-start = (bf16[256,4096]{1,0:T(8,128)(2,1)S(1)}, bf16[256,4096]{1,0:T(8,128)(2,1)}, u32[]{:S(2)}) copy-start(bf16[256,4096]{1,0:T(8,128)(2,1)} %hidden_ref.1) | copy-start | bytes 6291460
  3.2 1.2 %copy-start.1 = (bf16[1024,512]{1,0:T(8,128)(2,1)S(1)}, bf16[1024,512]{1,0:T(8,128)(2,1)}, u32[]{:S(2)}) copy-start(bf16[1024,512]{1,0:T(8,128)(2,1)} %weight_ref.1) | copy-start | bytes 3145732
  4.5 0.9 %copy-start.2 = (bf16[256,512]{1,0:T(8,128)(2,1)S(1)}, bf16[256,512]{1,0:T(8,128)(2,1)}, u32[]{:S(2)}) copy-start(bf16[256,512]{1,0:T(8,128)(2,1)} %keys_ref.1) | copy-start | bytes 786436
  5.4 0.8 %copy-start.3 = (bf16[16,2048]{1,0:T(8,128)(2,1)S(1)}, bf16[16,2048]{1,0:T(8,128)(2,1)}, u32[]{:S(2)}) copy-start(bf16[16,2048]{1,0:T(8,128)(2,1)} %queries_ref.1) | copy-start | bytes 196612
  6.3 0.8 copy-start.4
  7.0 0.7 copy-start.5
  7.7 0.7 copy-start.6

commit v2 on v1

--- a/solution.py
+++ b/solution.py
@@ -164,17 +164,23 @@
 
 def fused(
     n_dp,
+    hidden_hbm,
+    keys_hbm,
+    queries_hbm,
+    weight_hbm,
+    down_in_hbm,
+    up_hbm,
+    len_hbm,
+    partner_hbm,
+    loss_ref,
+    down_ref,
+    up_out_ref,
     hidden_ref,
     keys_ref,
     queries_ref,
-    weight_ref,
-    down_in_ref,
     up_ref,
     len_ref,
     partner_ref,
-    loss_ref,
-    down_ref,
-    up_out_ref,
     w_all,
     acc,
     low_t,
@@ -193,6 +199,7 @@
     w_sem,
     e_sem,
     g_sem,
+    load_sem,
 ):
     f32, bf16 = jnp.float32, jnp.bfloat16
     a, f = lax.axis_index("dp"), lax.axis_index("fsdp")
@@ -216,19 +223,31 @@
     rank, width = up_ref.shape
     emb_w = queries_ref.shape[1]
     groups = HEADS // KVH
-    half = weight_ref.shape[0] // 2
-    piece = (half + rank) // 2
+    half = weight_hbm.shape[0] // 2
+    tall = half + rank
+    edge = tall // 4 // 16 * 16
+    sizes = [edge, tall // 2 - edge, tall // 2 - edge, edge]
+    offsets = [0, edge, tall // 2, tall - edge]
     strings = emb_all.shape[0]
 
-    eye = (
-        lax.broadcasted_iota(jnp.int32, (rank, rank), 0)
-        == lax.broadcasted_iota(jnp.int32, (rank, rank), 1)
-    ).astype(bf16)
+    loads = []
+
+    def load(src, dst):
+        copy = pltpu.make_async_copy(src, dst, load_sem.at[len(loads)])
+        copy.start()
+        loads.append(copy)
+
     for h in range(2):
-        w_all[f, h, 0:half, :] = weight_ref[h * half : (h + 1) * half, :]
-        w_all[f, h, half : half + rank, :] = dot(
-            eye, down_in_ref[h * half : (h + 1) * half, :], 1, 1
-        ).astype(bf16)
+        load(weight_hbm.at[pl.ds(h * half, half), :], w_all.at[f, h, pl.ds(0, half), :])
+        load(down_in_hbm.at[:, pl.ds(h * half, half)], w_all.at[f, h, pl.ds(half, rank), :])
+    load(queries_hbm, queries_ref)
+    load(keys_hbm, keys_ref)
+    load(len_hbm, len_ref)
+    load(partner_hbm, partner_ref)
+    load(up_hbm, up_ref)
+    load(hidden_hbm, hidden_ref)
+    for copy in loads[:4]:
+        copy.wait()
     pl.semaphore_wait(barrier, len(peers))
 
     sends = []
@@ -255,20 +274,26 @@
             device_id_type=MESH,
         ).wait_recv()
 
-    def w_slot(s, h, c):
-        return w_all.at[s, h, pl.ds(c * piece, piece), :], w_sem.at[s, h, c]
-
-    def w_push(s, c, dev):
-        ref, sem = w_slot(s, k, c)
+    flip = z % 2
+    z_dev = ((z + 1 - 2 * flip) * 2 + k, f)
+
+    def w_slot(s, h, q):
+        start = offsets[q] + flip * (offsets[3 - q] - offsets[q])
+        here = pl.ds(pl.multiple_of(start, 16), sizes[q])
+        return w_all.at[s, h, here, :], w_sem.at[s, h, q + flip * (3 - 2 * q)]
+
+    def w_push(s, q, dev):
+        ref, sem = w_slot(s, k, q)
         push(ref, ref, sem, dev)
 
-    def w_arrive(s, h, c):
-        arrive(*w_slot(s, h, c))
-
-    w_push(f, 0, x_dev)
-    w_push(f, 1, y_dev)
-    w_push(f, 1, x_dev)
-    w_push(f, 0, y_dev)
+    def w_arrive(s, h, q):
+        arrive(*w_slot(s, h, q))
+
+    for q in range(3):
+        w_push(f, q, x_dev)
+        w_push(f, (1, 0, 2)[q], y_dev)
+    for copy in loads[4:]:
+        copy.wait()
 
     rows = groups * strs
     row_str = lax.broadcasted_iota(jnp.int32, (rows, strs), 0) % strs
@@ -300,30 +325,37 @@
 
     project(f, 0)
     project(f, 1)
-    w_arrive(xn, k, 0)
-    w_push(xn, 0, y_dev)
-    w_push(xn, 0, pair_dev)
-    w_arrive(yn, k, 1)
-    w_push(yn, 1, x_dev)
-    w_push(yn, 1, pair_dev)
-    w_arrive(xn, k, 1)
-    w_push(xn, 1, pair_dev)
-    w_arrive(yn, k, 0)
-    w_push(yn, 0, pair_dev)
+    for s, q, on in (
+        (xn, 0, (y_dev, z_dev)),
+        (yn, 1, (x_dev,)),
+        (yn, 0, (z_dev,)),
+        (xn, 1, ()),
+        (xn, 2, ()),
+        (yn, 2, ()),
+        (xn, 3, ()),
+        (yn, 3, ()),
+    ):
+        w_arrive(s, k, q)
+        for dev in on:
+            w_push(s, q, dev)
+        w_push(s, q, pair_dev)
     project(xn, k)
     project(yn, k)
+    for q in (0, 1):
+        w_arrive(dn, k, q)
+        w_push(dn, q, z_dev)
+        w_push(dn, q, pair_dev)
     for s in (xn, yn):
-        for c in range(2):
-            w_arrive(s, other, c)
+        for q in range(4):
+            w_arrive(s, other, q)
         project(s, other)
-    for c in range(2):
-        w_arrive(dn, k, c)
-        w_push(dn, c, pair_dev)
+    for q in (3, 2):
+        w_arrive(dn, k, q)
+        w_push(dn, q, pair_dev)
     project(dn, k)
-    for c in range(2):
-        w_arrive(dn, other, c)
+    for q in range(4):
+        w_arrive(dn, other, q)
     project(dn, other)
-
     up_f = up_ref[...].astype(f32)
     value = acc[...] + dot(low_t[...], up_f, 0, 0, HIGHEST)
     square = jnp.zeros((strs, 1), f32)
@@ -499,17 +531,24 @@
     f32, bf16 = jnp.float32, jnp.bfloat16
     tall = rank + 16
     vmem = pl.BlockSpec(memory_space=pltpu.VMEM)
+    hbm = pl.BlockSpec(memory_space=pltpu.HBM)
     blocks = n_dp * n_fsdp
     loss, down_t, up_grad = pl.pallas_call(
         functools.partial(fused, n_dp),
         out_shape=(
-            jax.ShapeDtypeStruct((8, LANES), f32),
+            jax.ShapeDtypeStruct((1, 1), f32),
             jax.ShapeDtypeStruct((rank, shard), f32),
             jax.ShapeDtypeStruct((rank, width), f32),
         ),
-        in_specs=[vmem] * 8,
+        in_specs=[hbm] * 8,
         out_specs=(vmem,) * 3,
         scratch_shapes=[
+            pltpu.VMEM(hidden.shape, bf16),
+            pltpu.VMEM(keys.shape, bf16),
+            pltpu.VMEM(queries.shape, bf16),
+            pltpu.VMEM(adapter_up.shape, bf16),
+            pltpu.VMEM((1, strs), jnp.int32),
+            pltpu.VMEM((1, strs), jnp.int32),
             pltpu.VMEM((n_fsdp, 2, shard // 2 + rank, width), bf16),
             pltpu.VMEM((tok, width), f32),
             pltpu.VMEM((rank, tok), f32),
@@ -525,19 +564,20 @@
             pltpu.VMEM((nz, tall, LANES), bf16),
             pltpu.VMEM((2, nz, tall, LANES), bf16),
             pltpu.SemaphoreType.DMA((64 + 4 * n_dp,)),
-            pltpu.SemaphoreType.DMA((n_fsdp, 2, 2)),
+            pltpu.SemaphoreType.DMA((n_fsdp, 2, 4)),
             pltpu.SemaphoreType.DMA((blocks,)),
             pltpu.SemaphoreType.DMA((5 + nz + n_dp,)),
+            pltpu.SemaphoreType.DMA((10,)),
         ],
         compiler_params=pltpu.CompilerParams(
-            collective_id=0, has_side_effects=True, vmem_limit_bytes=48 * 1024 * 1024
+            collective_id=0, has_side_effects=True, vmem_limit_bytes=63 * 1024 * 1024
         ),
     )(
         hidden,
         keys,
         queries,
         value_weight,
-        adapter_down,
+        adapter_down.T,
         adapter_up,
         lengths,
         partner.reshape(1, strs),

time: 79 us -> 76.5 us (0.968)
  local copies, waits for them, and re-layouts: 9.47 us -> 3.04 us
  Pallas kernels: 68.5 us -> 70.9 us
  between operations: 0.66 us -> 2.4 us
    unnamed x17 -> x2, local copies, waits for them, and re-layouts: 8.96 us -> 3.04 us
    pallas_call x1, Pallas kernels: 68.5 us -> 70.9 us  [fused_shards(): pl.pallas_call(functools.partial(fused, n_dp), out_shape=(jax.ShapeDtypeS...]
where the time goes in v2:
time: 76.5 us; the launch traced here: 76.3 us
  Pallas kernels  70.9 us (93%)
  local copies, waits for them, and re-layouts  3.04 us (4%)
  between operations  2.4 us (3%)
    pallas_call x1, Pallas kernels, fused_shards(): pl.pallas_call(functools.partial(fused, n_dp), out_shape=(jax.ShapeDtypeS...  70.9 us
    unnamed x2, local copies, waits for them, and re-layouts  3.04 us

profile of v2, /device:TPU:0, one launch (start us, length us, event | category | flops | bytes accessed | tf_op | source)
XLA Modules:
  0.0 76.3 jit_solution(15932106193619313855)
XLA Ops:
  0.6 70.9 %shard_map.103 = (f32[1,1]{1,0:T(1,128)}, f32[32,1024]{1,0:T(8,128)}, f32[32,512]{1,0:T(8,128)}) custom-call(bf16[256,4096]{1,0:T(8,128)(2,1)} %hidden_hbm.1, bf16[256,512]{1,0:T(8,128)(2,1)} %keys_hbm.1, bf16[16,2048]{1,0:T(8,128)(2,1)} %queries_hbm.1, bf16[1024,512]{1,0:T(8,128)(2,1)} %weight_hbm.1, bf16[32,1024]{1,0:T(8,128)(2,1)} %bitcast.5, ...), custom_call_target="tpu_custom_call" | custom-call | tf_op jit(solution)/shard_map/pallas_call | solution.py:536
  72.1 1.6 %copy.15 = f32[1024,32]{0,1:T(8,128)} copy(f32[1024,32]{0,1:T(8,128)} %bitcast.4) | data formatting | bytes 262144
  73.7 1.5 %copy.16 = f32[32,512]{1,0:T(8,128)} copy(f32[32,512]{1,0:T(8,128)} %get-tuple-element.14) | data formatting | bytes 131072

commit v3 on v2

--- a/solution.py
+++ b/solution.py
@@ -154,7 +154,7 @@
     rank, width = adapter_up.shape
     return (
         n_fsdp == 4
-        and n_dp % 2 == 0
+        and n_dp == 8
         and strings <= 1024
         and queries.shape[0] == 16
         and (rank // 16) * (width // LANES) == n_dp
@@ -211,7 +211,9 @@
     dn = (xn + 2) % 4
     pair_dev = (z * 2 + other, f)
     x_dev, y_dev, d_dev = (a, xn), (a, yn), (a, dn)
-    z_list = [(z + r) % nz for r in range(nz)]
+    upper = z // 2
+    inner = z + upper * (3 - 2 * z)
+    z_list = [z] + [t + upper * (3 - 2 * t) for t in (1 - inner, 2, 3)]
     z_devs = [(zz * 2 + k, f) for zz in z_list]
 
     barrier = pltpu.get_barrier_semaphore()
@@ -264,6 +266,13 @@
         copy.start()
         sends.append(copy)
 
+    drained = []
+
+    def drain():
+        for copy in sends[len(drained) :]:
+            copy.wait_send()
+            drained.append(copy)
+
     def arrive(dst, recv):
         pltpu.make_async_remote_copy(
             src_ref=dst,
@@ -289,9 +298,9 @@
     def w_arrive(s, h, q):
         arrive(*w_slot(s, h, q))
 
-    for q in range(3):
+    for q in range(2):
         w_push(f, q, x_dev)
-        w_push(f, (1, 0, 2)[q], y_dev)
+        w_push(f, 1 - q, y_dev)
     for copy in loads[4:]:
         copy.wait()
 
@@ -325,33 +334,31 @@
 
     project(f, 0)
     project(f, 1)
-    for s, q, on in (
-        (xn, 0, (y_dev, z_dev)),
-        (yn, 1, (x_dev,)),
-        (yn, 0, (z_dev,)),
-        (xn, 1, ()),
-        (xn, 2, ()),
-        (yn, 2, ()),
-        (xn, 3, ()),
-        (yn, 3, ()),
-    ):
+    def w_relay(s, q, on):
         w_arrive(s, k, q)
         for dev in on:
             w_push(s, q, dev)
         w_push(s, q, pair_dev)
+
+    w_relay(xn, 0, (y_dev, z_dev))
+    w_relay(yn, 1, (x_dev,))
+    w_push(f, 2, x_dev)
+    w_push(f, 2, y_dev)
+    w_relay(yn, 0, (z_dev,))
+    w_relay(xn, 1, ())
+    w_relay(dn, 0, (z_dev,))
+    w_relay(dn, 1, (z_dev,))
+    for q in (3, 2):
+        w_relay(xn, q, ())
+        w_relay(yn, q, ())
     project(xn, k)
     project(yn, k)
-    for q in (0, 1):
-        w_arrive(dn, k, q)
-        w_push(dn, q, z_dev)
-        w_push(dn, q, pair_dev)
     for s in (xn, yn):
         for q in range(4):
             w_arrive(s, other, q)
         project(s, other)
     for q in (3, 2):
-        w_arrive(dn, k, q)
-        w_push(dn, q, pair_dev)
+        w_relay(dn, q, ())
     project(dn, k)
     for q in range(4):
         w_arrive(dn, other, q)
@@ -402,18 +409,29 @@
         e_push(own_block, dev)
     for dev in (x_dev, y_dev, pair_dev):
         e_push(own_block, dev)
-    for r in range(1, nz):
+    drain()
+
+    def from_z(r, devs):
         blk = block_of(z_list[r], k, f)
         arrive(*blk)
-        for dev in (x_dev, y_dev, pair_dev):
+        for dev in devs:
             e_push(blk, dev)
-    for r in range(nz):
+
+    def from_plane(r):
         for s, relay in ((xn, y_dev), (yn, x_dev)):
             blk = block_of(z_list[r], k, s)
             arrive(*blk)
-            if (r % 2 == 0) == (s is xn):
+            if r < nz - 1 and (r % 2 == 0) == (s is xn):
                 e_push(blk, relay)
             e_push(blk, pair_dev)
+
+    from_z(1, (x_dev, y_dev, pair_dev))
+    from_plane(0)
+    from_z(2, (x_dev, y_dev, pair_dev))
+    from_plane(1)
+    from_z(3, (d_dev, x_dev, y_dev, pair_dev))
+    from_plane(2)
+    from_plane(3)
     for r in range(nz):
         blk = block_of(z_list[r], k, dn)
         arrive(*blk)
@@ -426,7 +444,7 @@
 
     def rows_of(i, loss):
         here = pl.ds(pl.multiple_of(i * step, step), step)
-        logits = dot(emb_all[here, 0:emb_w], emb_all[:, 0:emb_w], 1, 1) / sharpness_divisor
+        logits = dot(emb_all[here, 0:emb_w], emb_all[:, 0:emb_w], 1, 1) * (1.0 / sharpness_divisor)
         row = i * step + lax.broadcasted_iota(jnp.int32, (step, strings), 0)
         col = lax.broadcasted_iota(jnp.int32, (step, strings), 1)
         total = jnp.sum(jnp.where(row != col, jnp.exp(logits), 0.0), axis=1, keepdims=True)
@@ -441,7 +459,7 @@
     loss = lax.fori_loop(0, strings // step, rows_of, jnp.zeros((1, 1), f32))
     loss_ref[...] = jnp.broadcast_to(loss / strings, loss_ref.shape)
 
-    logits = dot(emb_all[:, 0:emb_w], emb, 1, 1) / sharpness_divisor
+    logits = dot(emb_all[:, 0:emb_w], emb, 1, 1) * (1.0 / sharpness_divisor)
     j = lax.broadcasted_iota(jnp.int32, (strings, strs), 0)
     i = mine + lax.broadcasted_iota(jnp.int32, (strings, strs), 1)
     expd = jnp.where(i != j, jnp.exp(logits), 0.0)
@@ -450,8 +468,8 @@
     code = emb_all[:, emb_w : emb_w + LANES].astype(f32)
     mate = code[:, 0:1] + 256.0 * code[:, 1:2]
     hit = jnp.where(mate == i.astype(f32), 1.0, 0.0)
-    row_grad = ((expd / own_total - own_hit) / sharpness_divisor).astype(bf16)
-    col_grad = ((expd / totals[:, 0:1] - hit) / sharpness_divisor).astype(bf16)
+    row_grad = ((expd / own_total - own_hit) * (1.0 / sharpness_divisor)).astype(bf16)
+    col_grad = ((expd / totals[:, 0:1] - hit) * (1.0 / sharpness_divisor)).astype(bf16)
     every = emb_all[:, 0:emb_w]
     grad_emb = dot(row_grad, every, 0, 0) + dot(col_grad, every, 0, 0)
     unit = unit_ref[...]
@@ -480,6 +498,7 @@
             msg[aa % 2, ff, aa // 2, rank : rank + 16, :] = up_part[r0 : r0 + 16, c0 : c0 + LANES]
 
     push(msg.at[other], got1, g_sem.at[0], pair_dev)
+    drain()
     arrive(got1, g_sem.at[0])
     sum1[...] = (msg[k].astype(f32) + got1[...].astype(f32)).astype(bf16)
     for n, (s, dev) in enumerate(((xn, x_dev), (yn, y_dev), (dn, d_dev))):
@@ -516,8 +535,7 @@
         up_out_ref[r0 : r0 + 16, c0 : c0 + LANES] = final[
             aa % 2, aa // 2, rank : rank + 16, :
         ].astype(f32)
-    for copy in sends:
-        copy.wait_send()
+    drain()
 
 
 def fused_shards(hidden, keys, queries, value_weight, adapter_down, adapter_up, lengths, partner):

time: 76.5 us -> 75.7 us (0.990)
  Pallas kernels: 70.9 us -> 70.1 us
    pallas_call x1, Pallas kernels: 70.9 us -> 70.1 us  [fused_shards(): pl.pallas_call(functools.partial(fused, n_dp), out_shape=(jax.ShapeDtypeS...]
where the time goes in v3:
time: 75.7 us; the launch traced here: 75.5 us
  Pallas kernels  70.1 us (93%)
  local copies, waits for them, and re-layouts  3.04 us (4%)
  between operations  2.4 us (3%)
    pallas_call x1, Pallas kernels, fused_shards(): pl.pallas_call(functools.partial(fused, n_dp), out_shape=(jax.ShapeDtypeS...  70.1 us
    unnamed x2, local copies, waits for them, and re-layouts  3.04 us

profile of v3, /device:TPU:0, one launch (start us, length us, event | category | flops | bytes accessed | tf_op | source)
XLA Modules:
  0.0 75.5 jit_solution(3123532504041618734)
XLA Ops:
  0.6 70.1 %shard_map.103 = (f32[1,1]{1,0:T(1,128)}, f32[32,1024]{1,0:T(8,128)}, f32[32,512]{1,0:T(8,128)}) custom-call(bf16[256,4096]{1,0:T(8,128)(2,1)} %hidden_hbm.1, bf16[256,512]{1,0:T(8,128)(2,1)} %keys_hbm.1, bf16[16,2048]{1,0:T(8,128)(2,1)} %queries_hbm.1, bf16[1024,512]{1,0:T(8,128)(2,1)} %weight_hbm.1, bf16[32,1024]{1,0:T(8,128)(2,1)} %bitcast.5, ...), custom_call_target="tpu_custom_call" | custom-call | tf_op jit(solution)/shard_map/pallas_call | solution.py:554
  71.4 1.6 %copy.15 = f32[1024,32]{0,1:T(8,128)} copy(f32[1024,32]{0,1:T(8,128)} %bitcast.4) | data formatting | bytes 262144
  72.9 1.5 %copy.16 = f32[32,512]{1,0:T(8,128)} copy(f32[32,512]{1,0:T(8,128)} %get-tuple-element.14) | data formatting | bytes 131072

commit v4 on v3

--- a/solution.py
+++ b/solution.py
@@ -483,10 +483,12 @@
             ],
             axis=0,
         )
-        acc[:, kv * HD : (kv + 1) * HD] = dot(probs[kv], g_kv, 0, 0, HIGHEST)
-    grad_value = acc[...]
-    up_part = dot(low_t[...], grad_value, 1, 0, HIGHEST).astype(bf16)
-    grad_low_t = dot(up_f, grad_value, 1, 1, HIGHEST).astype(bf16)
+        acc[:, kv * HD : (kv + 1) * HD] = dot(
+            probs[kv].astype(bf16), g_kv.astype(bf16), 0, 0
+        )
+    grad_value = acc[...].astype(bf16)
+    up_part = dot(low_t[...].astype(bf16), grad_value, 1, 0).astype(bf16)
+    grad_low_t = dot(up_ref[...], grad_value, 1, 1).astype(bf16)
 
     per_row = width // LANES
     span = n_dp * LANES

time: 75.7 us -> 74.6 us (0.985)
  Pallas kernels: 70.1 us -> 68.9 us
    pallas_call x1, Pallas kernels: 70.1 us -> 68.9 us  [fused_shards(): pl.pallas_call(functools.partial(fused, n_dp), out_shape=(jax.ShapeDtypeS...]
where the time goes in v4:
time: 74.6 us; the launch traced here: 74.4 us
  Pallas kernels  68.9 us (92%)
  local copies, waits for them, and re-layouts  3.04 us (4%)
  between operations  2.4 us (3%)
    pallas_call x1, Pallas kernels, fused_shards(): pl.pallas_call(functools.partial(fused, n_dp), out_shape=(jax.ShapeDtypeS...  68.9 us
    unnamed x2, local copies, waits for them, and re-layouts  3.04 us

profile of v4, /device:TPU:0, one launch (start us, length us, event | category | flops | bytes accessed | tf_op | source)
XLA Modules:
  0.0 74.4 jit_solution(393600815671105736)
XLA Ops:
  0.6 68.9 %shard_map.103 = (f32[1,1]{1,0:T(1,128)}, f32[32,1024]{1,0:T(8,128)}, f32[32,512]{1,0:T(8,128)}) custom-call(bf16[256,4096]{1,0:T(8,128)(2,1)} %hidden_hbm.1, bf16[256,512]{1,0:T(8,128)(2,1)} %keys_hbm.1, bf16[16,2048]{1,0:T(8,128)(2,1)} %queries_hbm.1, bf16[1024,512]{1,0:T(8,128)(2,1)} %weight_hbm.1, bf16[32,1024]{1,0:T(8,128)(2,1)} %bitcast.5, ...), custom_call_target="tpu_custom_call" | custom-call | tf_op jit(solution)/shard_map/pallas_call | solution.py:556
  70.2 1.6 %copy.15 = f32[1024,32]{0,1:T(8,128)} copy(f32[1024,32]{0,1:T(8,128)} %bitcast.4) | data formatting | bytes 262144
  71.8 1.5 %copy.16 = f32[32,512]{1,0:T(8,128)} copy(f32[32,512]{1,0:T(8,128)} %get-tuple-element.14) | data formatting | bytes 131072
